TPU v7x, 256 devices: a whole 4x4x8 slice. The times are simulated.
256 devices in a mesh: grp: 16 (over x, y), tp: 16 (over z, core).
Axes of the slice: x: 4, y: 4, z: 8, core: 2. Of those that a mesh axis runs over, the one named last changes fastest.
Arguments:
- tokens: bfloat16 [12288, 3584], P(('grp', 'tp')), parts along dimension 0, may hold values from -6 to 6
- counts: int32 [256], P(('grp', 'tp')), parts along dimension 0, may hold values from 16 to 48, as said below
- norm_gain: float32 [3584], replicated, may hold values from 0.1 to 1.9
- gate_weight: bfloat16 [3584, 9216], P(None, 'tp'), may hold values from -0.09375 to 0.09375
- up_weight: bfloat16 [3584, 9216], P(None, 'tp'), may hold values from -0.09375 to 0.09375
- down_weight: bfloat16 [9216, 3584], P('tp'), may hold values from -0.0625 to 0.0625
Outputs:
- mixed: bfloat16 [12288, 3584], P(('grp', 'tp')), parts along dimension 0
There are 16 independent parts, one for each index of `grp`. A program takes and returns all parts, laid end to end along the dimension named above; an argument that names none is the same for every part. Nothing has to cross between parts.
Inputs may be any that keep to these rules, and one draw needn't show every extreme that they name: `counts`: each device holds from 16 to 48 live requests in its first slots; in every group some device holds exactly 48 and another exactly 16.
All inputs are finite; a program needn't handle non-finite values.
Results may differ from a plain program's by a relative error of at most 0.023.
Values may be sent and summed in bfloat16 or wider, within the bound.
No kernel may reach another device: no remote copies, remote signals or barrier semaphores. Data moves between devices by JAX's collectives and lax.ppermute only.
A program may use at most 64 MiB of HBM per device.

v0:
```python
import jax
import jax.numpy as jnp
from jax import lax
from jax.sharding import PartitionSpec as P


def body(tokens, counts, norm_gain, gate_weight, up_weight, down_weight):
    slot_count = tokens.shape[0]
    widened = tokens.astype(jnp.float32)
    scale_row = lax.rsqrt(jnp.mean(widened * widened, axis=-1, keepdims=True) + 1e-06)
    normed = (widened * scale_row * norm_gain).astype(jnp.bfloat16)
    piece = lax.all_gather(normed, "tp", axis=0, tiled=True)
    gate = jnp.dot(piece, gate_weight, preferred_element_type=jnp.float32)
    up_part = jnp.dot(piece, up_weight, preferred_element_type=jnp.float32)
    hidden = (jax.nn.silu(gate) * up_part).astype(jnp.bfloat16)
    mine_rows = lax.psum_scatter(
        jnp.dot(hidden, down_weight, preferred_element_type=jnp.float32).astype(jnp.bfloat16),
        "tp",
        scatter_dimension=0,
        tiled=True,
    ).astype(jnp.float32)
    alive_mask = jnp.arange(slot_count, dtype=jnp.int32) < counts[0]
    return jnp.where(alive_mask[:, None], mine_rows, 0.0).astype(jnp.bfloat16)


def solution(mesh):
    in_specs = (
        P(("grp", "tp"), None),
        P(("grp", "tp")),
        P(),
        P(None, "tp"),
        P(None, "tp"),
        P("tp", None),
    )
    out_specs = P(("grp", "tp"), None)
    return jax.shard_map(body, mesh=mesh, in_specs=in_specs, out_specs=out_specs, check_vma=False)
```

profile of v0, /device:TPU:1, one launch (start us, length us, event | category | flops | bytes accessed | tf_op | source)
XLA Modules:
  0.0 148.6 jit_solution(4320535811709258528)
XLA Ops:
  6.5 0.0 all-gather.2.cloned.1.call-start
  6.5 1.1 fusion
  7.7 1.9 %fusion.2 = bf16[48,3584]{1,0:T(8,128)(2,1)} fusion(bf16[48,3584]{1,0:T(8,128)(2,1)} %param.6, f32[3584]{0:T(1024)} %param.8, f32[48]{0:T(128)S(1)} %add_rsqrt_fusion), kind=kLoop, calls=%fused_computation.6 | loop fusion | flops 688128 | bytes 702656 | tf_op jit(solution)/shard_map/convert_element_type | solution.py:11
  9.6 0.0 all-gather.2.cloned.1.call-update
  9.6 0.0 reduce-scatter.2.cloned.1.call-start
  9.6 48.5 %all-gather.2.cloned.1.call-done = bf16[768,3584]{1,0:T(8,128)(2,1)} async-done(((bf16[48,3584]{1,0:T(8,128)(2,1)}), bf16[768,3584]{1,0:T(8,128)(2,1)}) %all-gather.2.cloned.1.call-update) | async-done | bytes 5505040 | tf_op jit(solution)/shard_map/all_gather | solution.py:12
  58.2 6.8 %fusion.4 = f32[768,576]{0,1:T(8,128)S(1)} fusion(bf16[768,3584]{1,0:T(8,128)(2,1)} %all-gather.2.cloned.1.call-done, bf16[3584,576]{0,1:T(8,128)(2,1)} %param.9), kind=kOutput, calls=%fused_computation.11 | convolution fusion | flops 3170893824 | bytes 11403264 | tf_op jit(solution)/shard_map/dot_general | solution.py:13
  65.0 14.9 %convolution_convert_fusion = bf16[768,3584]{1,0:T(8,128)(2,1)} fusion(bf16[576,3584]{1,0:T(8,128)(2,1)} %param.11, f32[768,576]{0,1:T(8,128)S(1)} %fusion.4, bf16[768,3584]{1,0:T(8,128)(2,1)} %all-gather.2.cloned.1.call-done, bf16[3584,576]{0,1:T(8,128)(2,1)} %param.10), kind=kOutput, calls=%fused_computation | convolution fusion | flops 6347194368 | bytes 21037056 | tf_op jit(solution)/shard_map/dot_general | solution.py:17
  79.9 0.0 reduce-scatter.2.cloned.1.call-update
  80.6 59.3 %reduce-scatter.2.cloned.1.call-done = bf16[48,3584]{1,0:T(8,128)(2,1)} async-done(((bf16[768,3584]{1,0:T(8,128)(2,1)}), bf16[48,3584]{1,0:T(8,128)(2,1)}) %reduce-scatter.2.cloned.1.call-update) | async-done | bytes 344080 | tf_op jit(solution)/shard_map/reduce_scatter | solution.py:16
  139.9 1.8 %select_convert_fusion = bf16[48,3584]{1,0:T(8,128)(2,1)} fusion(bf16[48,3584]{1,0:T(8,128)(2,1)} %reduce-scatter.2.cloned.1.call-done, pred[48]{0:T(512)(128)(4,1)S(1)} %iota_compare_fusion), kind=kLoop, calls=%fused_computation.7 | loop fusion | flops 516096 | bytes 688176 | tf_op jit(solution)/shard_map/convert_element_type | solution.py:23
  (2 shorter events, 0.0 us)
Async XLA Ops:
  6.5 51.6 %all-gather.2.cloned.1.call-start = ((), (), s32[]{:S(2)}) async-start(), calls=%async_computation.1 | async-start | bytes 5849088 | tf_op jit(solution)/shard_map/all_gather | solution.py:12
  9.6 130.3 %reduce-scatter.2.cloned.1.call-start = ((), (), s32[]{:S(2)}) async-start(), calls=%async_computation.2 | async-start | bytes 5849088 | tf_op jit(solution)/shard_map/reduce_scatter | solution.py:16
Sparse Core Ops, SparseCore 0:
  9.7 48.4 all-gather.1
  80.0 59.7 reduce-scatter.1
where the time goes:
time: 151 us; the launch traced here: 149 us
  waiting for transfers between devices  108 us (72%)
  matrix products  21.7 us (14%)
  between operations  14.1 us (9%)
  other arithmetic  4.86 us (3%)
    reduce_scatter x1, waiting for transfers between devices, body(): lax.psum_scatter(jnp.dot(hidden, down_weight, preferred_element_type=jnp....  59.3 us
    all_gather x1, waiting for transfers between devices, body(): piece = lax.all_gather(normed, 'tp', axis=0, tiled=True)  48.5 us
    dot_general x1, matrix products, body(): jnp.dot(hidden, down_weight, preferred_element_type=jnp.float32)  14.9 us
    dot_general x1, matrix products, body(): gate = jnp.dot(piece, gate_weight, preferred_element_type=jnp.float32)  6.79 us
  transfers between devices with their start and end apart: 2, of which 2 were waited for; matrix products, arithmetic and copies ran while one was open for 0% of the time, Pallas kernels for 0%

commit v1 on v0

v1 whole, which is shorter than its diff:
```python
import jax
import jax.numpy as jnp
from jax import lax
from jax.experimental import pallas as pl
from jax.experimental.pallas import tpu as pltpu
from jax.sharding import PartitionSpec as P

CHUNKS = 3
HOP_BYTES = 9_000_000
IN_VMEM = pl.BlockSpec(memory_space=pltpu.VMEM)


def local(kernel, shape, operands, specs=None, bytes_accessed=HOP_BYTES):
    return pl.pallas_call(
        kernel,
        out_shape=jax.ShapeDtypeStruct(shape, jnp.bfloat16),
        in_specs=specs or [IN_VMEM] * len(operands),
        out_specs=IN_VMEM,
        compiler_params=pltpu.CompilerParams(vmem_limit_bytes=3 << 20),
        cost_estimate=pl.CostEstimate(flops=0, bytes_accessed=bytes_accessed, transcendentals=0),
    )(*operands)


def normalize(tokens, gain):
    slots, width = tokens.shape

    def kernel(tokens_ref, gain_ref, normed_ref):
        for at in range(0, slots, 16):
            rows = pl.ds(at, 16)
            widened = tokens_ref[rows, :].astype(jnp.float32)
            scale_row = lax.rsqrt(jnp.sum(widened * widened, axis=-1, keepdims=True) / width + 1e-06)
            normed_ref[rows, :] = (widened * scale_row * gain_ref[...]).astype(normed_ref.dtype)

    return local(kernel, tokens.shape, (tokens, gain.reshape(1, width)))


def join(size, *terms):
    spans = [(at, rows) for _, at, rows in terms]

    def kernel(*refs):
        cut = min(rows for _, rows in spans)
        for low, high in ((0, cut), (cut, size)):
            if low < high:
                total = None
                for ref, (at, rows) in zip(refs, spans):
                    if rows >= high:
                        value = ref[pl.ds(at + low, high - low), :].astype(jnp.float32)
                        total = value if total is None else total + value
                refs[-1][pl.ds(low, high - low), :] = total.astype(refs[-1].dtype)

    return local(kernel, (size, terms[0][0].shape[1]), [array for array, _, _ in terms])


def body(tokens, counts, norm_gain, gate_weight, up_weight, down_weight):
    slots, width = tokens.shape
    members = lax.axis_size("tp")
    chips = members // 2
    part = slots // CHUNKS
    both = 2 * part

    swap_pairs = [(i, i ^ 1) for i in range(members)]
    ring_pairs = [(2 * z, 2 * ((z + 1) % chips)) for z in range(chips)]
    ring_pairs += [(2 * z + 1, 2 * ((z - 1) % chips) + 1) for z in range(chips)]

    def swap(value):
        return lax.ppermute(value, "tp", swap_pairs)

    def ring(value):
        return lax.ppermute(value, "tp", ring_pairs)

    f32 = jnp.float32
    bf16 = jnp.bfloat16
    token = counts

    def order(*values):
        nonlocal token
        token, *values = lax.optimization_barrier((token, *values))
        return values if len(values) > 1 else values[0]

    def concat(*values):
        return order(jnp.concatenate(order(*values), 0))

    batch = {}

    def gate_of(name):
        rows, weight = order(batch[name], gate_weight)
        batch[name] = rows, order(jnp.dot(rows, weight, preferred_element_type=f32))

    def hidden_of(name):
        rows, gate, weight = order(*batch[name], up_weight)
        up_part = jnp.dot(rows, weight, preferred_element_type=f32)
        batch[name] = order((jax.nn.silu(gate) * up_part).astype(bf16))

    def partial_of(name):
        hidden, weight = order(batch[name], down_weight)
        batch[name] = order(jnp.dot(hidden, weight, preferred_element_type=f32).astype(bf16))

    chunks = range(CHUNKS)
    normed = order(normalize(*order(tokens, norm_gain)))
    swapped = order(swap(normed))
    own, flight = [], []
    for i in chunks:
        rows = slice(i * part, (i + 1) * part)
        own.append(concat(normed[rows], swapped[rows]))
        flight.append(ring(own[i]))

    mine = {}
    other = {}

    def arrive(hop, i):
        block = order(flight[i])
        mine[hop, i] = block
        if hop < 3:
            flight[i] = ring(block)
        elif hop == 3:
            flight[i] = ring(block[:part])

    arrive(1, 0)
    arrive(1, 1)
    arrive(1, 2)
    other[1] = swap(concat(*[mine[1, i] for i in chunks]))
    arrive(2, 0)
    other[1] = order(other[1])
    batch["a"] = concat(*own, *[mine[1, i] for i in chunks], other[1][:2 * both])
    gate_of("a")
    arrive(2, 1)
    hidden_of("a")
    arrive(2, 2)
    other[2] = swap(concat(*[mine[2, i] for i in chunks]))
    partial_of("a")
    arrive(3, 0)
    moved_1 = swap(batch["a"][3 * both:6 * both])
    other[2] = order(other[2])
    batch["b"] = concat(other[1][2 * both:], other[2], *[mine[2, i] for i in chunks], mine[3, 0])
    gate_of("b")
    arrive(3, 1)
    moved_1 = order(moved_1)
    hidden_of("b")
    arrive(3, 2)
    other[3] = swap(concat(*[mine[3, i] for i in chunks]))
    partial_of("b")
    moved_2 = swap(batch["b"][4 * both:])
    other[3] = order(other[3])
    arrive(4, 0)
    moved_2 = order(moved_2)
    arrive(4, 1)
    arrive(4, 2)
    fourth = concat(*[mine[4, i] for i in chunks])
    other[4] = order(swap(fourth))
    batch["c"] = concat(other[3], mine[3, 1], mine[3, 2], fourth, other[4])
    gate_of("c")
    hidden_of("c")
    partial_of("c")
    moved_4 = swap(batch["c"][5 * both:5 * both + 3 * part])
    moved_3 = swap(batch["c"][3 * both:5 * both])
    moved_4 = order(moved_4)

    def depart(hop, i):
        size = part if hop == 4 else both
        terms = []
        if hop == 4:
            terms = [(batch["c"], 5 * both + 3 * part + i * part, part), (moved_4, i * part, part)]
        elif hop == 3:
            there = (moved_2, 3 * both, both) if i == 0 else (moved_3, (i - 1) * both, both)
            terms = [(batch["c"], i * both, both), there, (flight[i], 0, part)]
        elif hop == 2:
            terms = [(batch["b"], (1 + i) * both, both), (moved_2, i * both, both), (flight[i], 0, both)]
        elif hop == 1:
            here = (batch["b"], 0, both) if i == 2 else (batch["a"], (6 + i) * both, both)
            terms = [here, (moved_1, i * both, both), (flight[i], 0, both)]
        arrays = order(*[array for array, _, _ in terms])
        terms = [(array, at, rows) for array, (_, at, rows) in zip(arrays, terms)]
        flight[i] = ring(order(join(size, *terms)))

    for i in chunks:
        depart(4, i)
    moved_3 = order(moved_3)
    for hop in (3, 2, 1):
        for i in chunks:
            depart(hop, i)
    given = []
    for i in chunks:
        carry, mixed = order(flight[i], batch["a"])
        flight[i] = carry
        given.append(swap(order(join(part, (mixed, i * both + part, part), (carry, 0, part)))))
    done = []
    for i in chunks:
        carry, mixed, gift = order(flight[i], batch["a"], given[i])
        done.append(carry[part:].astype(f32) + mixed[i * both:i * both + part].astype(f32) + gift.astype(f32))
    alive = jnp.arange(slots, dtype=jnp.int32) < token[0]
    return jnp.where(alive[:, None], jnp.concatenate(done, 0), 0.0).astype(bf16)


def solution(mesh):
    in_specs = (
        P(("grp", "tp"), None),
        P(("grp", "tp")),
        P(),
        P(None, "tp"),
        P(None, "tp"),
        P("tp", None),
    )
    out_specs = P(("grp", "tp"), None)
    return jax.shard_map(body, mesh=mesh, in_specs=in_specs, out_specs=out_specs, check_vma=False)
```

time: 151 us -> 103 us (0.68); the launches traced: 149 us -> 103 us
  waiting for transfers between devices: 108 us -> 26.8 us
  starting transfers between devices: 0.04 us -> 54.6 us
  between operations: 14.1 us -> 1.1 us
  matrix products: 21.7 us -> 12.4 us
  local copies, waits for them, and re-layouts: 0 us -> 5.46 us
  other arithmetic: 4.86 us -> 1.22 us
    reduce_scatter x1 -> x0, waiting for transfers between devices: 59.3 us -> none  [body(): lax.psum_scatter(jnp.dot(hidden, down_weight, preferred_element_type=jnp....]
    ppermute x0 -> x36, starting transfers between devices: none -> 54.6 us  [the longest x24 33.1 us: ring(): return lax.ppermute(value, 'tp', ring_pairs)]
    all_gather x1 -> x0, waiting for transfers between devices: 48.5 us -> none  [body(): piece = lax.all_gather(normed, 'tp', axis=0, tiled=True)]
    ppermute x0 -> x36, waiting for transfers between devices: none -> 26.8 us  [the longest x24 22.1 us: ring(): return lax.ppermute(value, 'tp', ring_pairs)]
    dot_general x2 -> x9, matrix products: 21.7 us -> 12.4 us  [the longest x3 4.84 us: partial_of(): jnp.dot(hidden, weight, preferred_element_type=f32).astype(bf16)]
    unnamed x0 -> x25, local copies, waits for them, and re-layouts: none -> 4.39 us
    convert_element_type x2 -> x1, other arithmetic: 3.7 us -> 0.86 us  [body(): return jnp.where(alive[:, None], jnp.concatenate(done, 0), 0.0).astype(bf16)]
  transfers between devices with their start and end apart: 2 -> 36, of which waited for: 2 -> 20; matrix products, arithmetic and copies ran while one was open for 0% -> 7% of each run, Pallas kernels for 0% -> 1%
where the time goes in v1:
time: 103 us
  starting transfers between devices  54.6 us (53%)
  waiting for transfers between devices  26.8 us (26%)
  matrix products  12.4 us (12%)
  local copies, waits for them, and re-layouts  5.46 us (5%)
  other arithmetic  1.22 us (1%)
  Pallas kernels  1.1 us (1%)
  between operations  1.1 us (1%)
    ppermute x24, starting transfers between devices, ring(): return lax.ppermute(value, 'tp', ring_pairs)  33.1 us
    ppermute x24, waiting for transfers between devices, ring(): return lax.ppermute(value, 'tp', ring_pairs)  22.1 us
    ppermute x12, starting transfers between devices, swap(): return lax.ppermute(value, 'tp', swap_pairs)  21.6 us
    dot_general x3, matrix products, partial_of(): jnp.dot(hidden, weight, preferred_element_type=f32).astype(bf16)  4.84 us
    ppermute x12, waiting for transfers between devices, swap(): return lax.ppermute(value, 'tp', swap_pairs)  4.7 us
    unnamed x25, local copies, waits for them, and re-layouts  4.39 us
    dot_general x3, matrix products, gate_of(): jnp.dot(rows, weight, preferred_element_type=f32)  3.78 us
    dot_general x3, matrix products, hidden_of(): up_part = jnp.dot(rows, weight, preferred_element_type=f32)  3.77 us
  transfers between devices with their start and end apart: 36, of which 20 were waited for; matrix products, arithmetic and copies ran while one was open for 7% of the time, Pallas kernels for 1%

profile of v1, /device:TPU:1, one launch (start us, length us, event | category | flops | bytes accessed | tf_op | source)
XLA Modules:
  0.0 102.6 jit_solution(15567889308123880934)
XLA Ops:
  1.9 3.3 %collective-permute-start = (bf16[48,3584]{1,0:T(8,128)(2,1)S(1)}, bf16[48,3584]{1,0:T(8,128)(2,1)S(1)}, u32[]{:S(2)}, u32[]{:S(2)}) collective-permute-start(bf16[48,3584]{1,0:T(8,128)(2,1)S(1)} %shard_map.64), channel_id=1, source_target_pairs={{0,1},{1,0},{2,3},{3,2},{4,5},{5,4},{6,7},{7,6},{8,9},{9,8},{10,11... | collective-permute-start | bytes 1032200 | tf_op jit(solution)/shard_map/ppermute | solution.py:66
  6.6 3.9 %collective-permute-start.1 = (bf16[32,3584]{1,0:T(8,128)(2,1)S(1)}, bf16[32,3584]{1,0:T(8,128)(2,1)S(1)}, u32[]{:S(2)}, u32[]{:S(2)}) collective-permute-start(bf16[32,3584]{1,0:T(8,128)(2,1)S(1)} %pad_maximum_fusion.4), channel_id=1, source_target_pairs={{0,2},{2,4},{4,6},{6,8},{8,10},{10,12},{12,14},{14,0},{1,15},{3,1}... | collective-permute-start | bytes 688136 | tf_op jit(solution)/shard_map/ppermute | solution.py:69
  13.5 2.5 %collective-permute-done.2 = bf16[32,3584]{1,0:T(8,128)(2,1)S(1)} collective-permute-done((bf16[32,3584]{1,0:T(8,128)(2,1)S(1)}, bf16[32,3584]{1,0:T(8,128)(2,1)S(1)}, u32[]{:S(2)}, u32[]{:S(2)}) %collective-permute-start.2) | collective-permute-done | bytes 229408 | tf_op jit(solution)/shard_map/ppermute | solution.py:69
  15.9 2.5 %collective-permute-done.3 = bf16[32,3584]{1,0:T(8,128)(2,1)S(1)} collective-permute-done((bf16[32,3584]{1,0:T(8,128)(2,1)S(1)}, bf16[32,3584]{1,0:T(8,128)(2,1)S(1)}, u32[]{:S(2)}, u32[]{:S(2)}) %collective-permute-start.3) | collective-permute-done | bytes 229408 | tf_op jit(solution)/shard_map/ppermute | solution.py:69
  18.4 1.8 %collective-permute-start.5 = (bf16[96,3584]{1,0:T(8,128)(2,1)S(1)}, bf16[96,3584]{1,0:T(8,128)(2,1)S(1)}, u32[]{:S(2)}, u32[]{:S(2)}) collective-permute-start(bf16[96,3584]{1,0:T(8,128)(2,1)S(1)} %pad_maximum_fusion), channel_id=1, source_target_pairs={{0,1},{1,0},{2,3},{3,2},{4,5},{5,4},{6,7},{7,6},{8,9},{9,8},{10,11... | collective-permute-start | bytes 2064392 | tf_op jit(solution)/shard_map/ppermute | solution.py:66
  20.2 1.7 %collective-permute-start.4 = (bf16[32,3584]{1,0:T(8,128)(2,1)S(1)}, bf16[32,3584]{1,0:T(8,128)(2,1)S(1)}, u32[]{:S(2)}, u32[]{:S(2)}) collective-permute-start(bf16[32,3584]{1,0:T(8,128)(2,1)S(1)} %collective-permute-done.1), channel_id=1, source_target_pairs={{0,2},{2,4},{4,6},{6,8},{8,10},{10,12},{12,14},{14,0},{1,15},{3,1}... | collective-permute-start | bytes 688136 | tf_op jit(solution)/shard_map/ppermute | solution.py:69
  23.4 2.0 %collective-permute-done.4 = bf16[32,3584]{1,0:T(8,128)(2,1)S(1)} collective-permute-done((bf16[32,3584]{1,0:T(8,128)(2,1)S(1)}, bf16[32,3584]{1,0:T(8,128)(2,1)S(1)}, u32[]{:S(2)}, u32[]{:S(2)}) %collective-permute-start.4) | collective-permute-done | bytes 229408 | tf_op jit(solution)/shard_map/ppermute | solution.py:69
  25.6 2.2 %copy-done.3 = bf16[3584,576]{0,1:T(8,128)(2,1)S(1)} copy-done((bf16[3584,576]{0,1:T(8,128)(2,1)S(1)}, bf16[3584,576]{0,1:T(8,128)(2,1)}, u32[]{:S(2)}) %copy-start.3) | copy-done | bytes 4128792
  31.3 2.2 %collective-permute-start.9 = (bf16[96,3584]{1,0:T(8,128)(2,1)S(1)}, bf16[96,3584]{1,0:T(8,128)(2,1)S(1)}, u32[]{:S(2)}, u32[]{:S(2)}) collective-permute-start(bf16[96,3584]{1,0:T(8,128)(2,1)S(1)} %pad_maximum_fusion.1), channel_id=1, source_target_pairs={{0,1},{1,0},{2,3},{3,2},{4,5},{5,4},{6,7},{7,6},{8,9},{9,8},{10,11... | collective-permute-start | bytes 2064392 | tf_op jit(solution)/shard_map/ppermute | solution.py:66
  38.8 2.4 %collective-permute-start.11 = (bf16[96,3584]{1,0:T(8,128)(2,1)S(1)}, bf16[96,3584]{1,0:T(8,128)(2,1)S(1)}, u32[]{:S(2)}, u32[]{:S(2)}) collective-permute-start(bf16[96,3584]{1,0:T(8,128)(2,1)S(1)} %slice.71), channel_id=1, source_target_pairs={{0,1},{1,0},{2,3},{3,2},{4,5},{5,4},{6,7},{7,6},{8,9},{9,8},{10,11... | collective-permute-start | bytes 2064392 | tf_op jit(solution)/shard_map/ppermute | solution.py:66
  44.3 1.6 %convolution_convert_fusion.1.refs_0_ = bf16[256,3584]{1,0:T(8,128)(2,1)S(1)} fusion(bf16[256,576]{0,1:T(8,128)(2,1)S(1)} %fusion.1, bf16[576,3584]{1,0:T(8,128)(2,1)S(1)} %copy-done.1), kind=kOutput, calls=%fused_computation.1 | convolution fusion | flops 1057882112 | bytes 6258688 | tf_op jit(solution)/shard_map/dot_general | solution.py:96
  46.0 1.6 %collective-permute-start.15 = (bf16[128,3584]{1,0:T(8,128)(2,1)S(1)}, bf16[128,3584]{1,0:T(8,128)(2,1)S(1)}, u32[]{:S(2)}, u32[]{:S(2)}) collective-permute-start(bf16[128,3584]{1,0:T(8,128)(2,1)S(1)} %slice.73), channel_id=1, source_target_pairs={{0,1},{1,0},{2,3},{3,2},{4,5},{5,4},{6,7},{7,6},{8,9},{9,8},{10,11... | collective-permute-start | bytes 2752520 | tf_op jit(solution)/shard_map/ppermute | solution.py:66
  48.0 2.2 %collective-permute-start.17 = (bf16[16,3584]{1,0:T(8,128)(2,1)S(1)}, bf16[16,3584]{1,0:T(8,128)(2,1)S(1)}, u32[]{:S(2)}, u32[]{:S(2)}) collective-permute-start(bf16[16,3584]{1,0:T(8,128)(2,1)S(1)} %slice.75), channel_id=1, source_target_pairs={{0,2},{2,4},{4,6},{6,8},{8,10},{10,12},{12,14},{14,0},{1,15},{3,1}... | collective-permute-start | bytes 344072 | tf_op jit(solution)/shard_map/ppermute | solution.py:69
  54.2 2.6 %collective-permute-start.18 = (bf16[48,3584]{1,0:T(8,128)(2,1)S(1)}, bf16[48,3584]{1,0:T(8,128)(2,1)S(1)}, u32[]{:S(2)}, u32[]{:S(2)}) collective-permute-start(bf16[48,3584]{1,0:T(8,128)(2,1)S(1)} %pad_maximum_fusion.3), channel_id=1, source_target_pairs={{0,1},{1,0},{2,3},{3,2},{4,5},{5,4},{6,7},{7,6},{8,9},{9,8},{10,11... | collective-permute-start | bytes 1032200 | tf_op jit(solution)/shard_map/ppermute | solution.py:66
  68.0 2.0 %collective-permute-start.24 = (bf16[32,3584]{1,0:T(8,128)(2,1)S(1)}, bf16[32,3584]{1,0:T(8,128)(2,1)S(1)}, u32[]{:S(2)}, u32[]{:S(2)}) collective-permute-start(bf16[32,3584]{1,0:T(8,128)(2,1)S(1)} %shard_map.68), channel_id=1, source_target_pairs={{0,2},{2,4},{4,6},{6,8},{8,10},{10,12},{12,14},{14,0},{1,15},{3,1}... | collective-permute-start | bytes 688136 | tf_op jit(solution)/shard_map/ppermute | solution.py:69
  73.3 2.9 %collective-permute-start.27 = (bf16[32,3584]{1,0:T(8,128)(2,1)S(1)}, bf16[32,3584]{1,0:T(8,128)(2,1)S(1)}, u32[]{:S(2)}, u32[]{:S(2)}) collective-permute-start(bf16[32,3584]{1,0:T(8,128)(2,1)S(1)} %shard_map.71), channel_id=1, source_target_pairs={{0,2},{2,4},{4,6},{6,8},{8,10},{10,12},{12,14},{14,0},{1,15},{3,1}... | collective-permute-start | bytes 688136 | tf_op jit(solution)/shard_map/ppermute | solution.py:69
  76.4 2.4 %collective-permute-start.28 = (bf16[32,3584]{1,0:T(8,128)(2,1)S(1)}, bf16[32,3584]{1,0:T(8,128)(2,1)S(1)}, u32[]{:S(2)}, u32[]{:S(2)}) collective-permute-start(bf16[32,3584]{1,0:T(8,128)(2,1)S(1)} %shard_map.72), channel_id=1, source_target_pairs={{0,2},{2,4},{4,6},{6,8},{8,10},{10,12},{12,14},{14,0},{1,15},{3,1}... | collective-permute-start | bytes 688136 | tf_op jit(solution)/shard_map/ppermute | solution.py:69
  78.8 2.4 %collective-permute-start.29 = (bf16[32,3584]{1,0:T(8,128)(2,1)S(1)}, bf16[32,3584]{1,0:T(8,128)(2,1)S(1)}, u32[]{:S(2)}, u32[]{:S(2)}) collective-permute-start(bf16[32,3584]{1,0:T(8,128)(2,1)S(1)} %shard_map.73), channel_id=1, source_target_pairs={{0,2},{2,4},{4,6},{6,8},{8,10},{10,12},{12,14},{14,0},{1,15},{3,1}... | collective-permute-start | bytes 688136 | tf_op jit(solution)/shard_map/ppermute | solution.py:69
  81.3 1.8 %collective-permute-done.28.refs_2_ = bf16[32,3584]{1,0:T(8,128)(2,1)S(1)} collective-permute-done((bf16[32,3584]{1,0:T(8,128)(2,1)S(1)}, bf16[32,3584]{1,0:T(8,128)(2,1)S(1)}, u32[]{:S(2)}, u32[]{:S(2)}) %collective-permute-start.28) | collective-permute-done | bytes 229408 | tf_op jit(solution)/shard_map/ppermute | solution.py:69
  83.1 2.9 %collective-permute-start.30 = (bf16[32,3584]{1,0:T(8,128)(2,1)S(1)}, bf16[32,3584]{1,0:T(8,128)(2,1)S(1)}, u32[]{:S(2)}, u32[]{:S(2)}) collective-permute-start(bf16[32,3584]{1,0:T(8,128)(2,1)S(1)} %shard_map.74), channel_id=1, source_target_pairs={{0,2},{2,4},{4,6},{6,8},{8,10},{10,12},{12,14},{14,0},{1,15},{3,1}... | collective-permute-start | bytes 688136 | tf_op jit(solution)/shard_map/ppermute | solution.py:69
  86.4 2.2 %collective-permute-start.32 = (bf16[32,3584]{1,0:T(8,128)(2,1)S(1)}, bf16[32,3584]{1,0:T(8,128)(2,1)S(1)}, u32[]{:S(2)}, u32[]{:S(2)}) collective-permute-start(bf16[32,3584]{1,0:T(8,128)(2,1)S(1)} %shard_map.76), channel_id=1, source_target_pairs={{0,2},{2,4},{4,6},{6,8},{8,10},{10,12},{12,14},{14,0},{1,15},{3,1}... | collective-permute-start | bytes 688136 | tf_op jit(solution)/shard_map/ppermute | solution.py:69
  88.9 2.4 %collective-permute-done.31.refs_1_ = bf16[32,3584]{1,0:T(8,128)(2,1)S(1)} collective-permute-done((bf16[32,3584]{1,0:T(8,128)(2,1)S(1)}, bf16[32,3584]{1,0:T(8,128)(2,1)S(1)}, u32[]{:S(2)}, u32[]{:S(2)}) %collective-permute-start.31) | collective-permute-done | bytes 229408 | tf_op jit(solution)/shard_map/ppermute | solution.py:69
  91.4 2.4 %collective-permute-done.32.refs_1_ = bf16[32,3584]{1,0:T(8,128)(2,1)S(1)} collective-permute-done((bf16[32,3584]{1,0:T(8,128)(2,1)S(1)}, bf16[32,3584]{1,0:T(8,128)(2,1)S(1)}, u32[]{:S(2)}, u32[]{:S(2)}) %collective-permute-start.32) | collective-permute-done | bytes 229408 | tf_op jit(solution)/shard_map/ppermute | solution.py:69
  93.8 6.2 %collective-permute-start.33 = (bf16[16,3584]{1,0:T(8,128)(2,1)S(1)}, bf16[16,3584]{1,0:T(8,128)(2,1)S(1)}, u32[]{:S(2)}, u32[]{:S(2)}) collective-permute-start(bf16[16,3584]{1,0:T(8,128)(2,1)S(1)} %shard_map.77), channel_id=1, source_target_pairs={{0,1},{1,0},{2,3},{3,2},{4,5},{5,4},{6,7},{7,6},{8,9},{9,8},{10,11... | collective-permute-start | bytes 344072 | tf_op jit(solution)/shard_map/ppermute | solution.py:66
  (125 shorter events, 41.4 us)
Async XLA Ops:
  6.6 6.9 %collective-permute-start.1 = (bf16[32,3584]{1,0:T(8,128)(2,1)S(1)}, bf16[32,3584]{1,0:T(8,128)(2,1)S(1)}, u32[]{:S(2)}, u32[]{:S(2)}) collective-permute-start(bf16[32,3584]{1,0:T(8,128)(2,1)S(1)} %pad_maximum_fusion.4), channel_id=1, source_target_pairs={{0,2},{2,4},{4,6},{6,8},{8,10},{10,12},{12,14},{14,0},{1,15},{3,1}... | collective-permute-start | bytes 688136 | tf_op jit(solution)/shard_map/ppermute | solution.py:69
  10.5 5.4 %collective-permute-start.2 = (bf16[32,3584]{1,0:T(8,128)(2,1)S(1)}, bf16[32,3584]{1,0:T(8,128)(2,1)S(1)}, u32[]{:S(2)}, u32[]{:S(2)}) collective-permute-start(bf16[32,3584]{1,0:T(8,128)(2,1)S(1)} %pad_maximum_fusion.5), channel_id=1, source_target_pairs={{0,2},{2,4},{4,6},{6,8},{8,10},{10,12},{12,14},{14,0},{1,15},{3,1}... | collective-permute-start | bytes 688136 | tf_op jit(solution)/shard_map/ppermute | solution.py:69
  11.3 7.1 %collective-permute-start.3 = (bf16[32,3584]{1,0:T(8,128)(2,1)S(1)}, bf16[32,3584]{1,0:T(8,128)(2,1)S(1)}, u32[]{:S(2)}, u32[]{:S(2)}) collective-permute-start(bf16[32,3584]{1,0:T(8,128)(2,1)S(1)} %pad_maximum_fusion.6), channel_id=1, source_target_pairs={{0,2},{2,4},{4,6},{6,8},{8,10},{10,12},{12,14},{14,0},{1,15},{3,1}... | collective-permute-start | bytes 688136 | tf_op jit(solution)/shard_map/ppermute | solution.py:69
  18.4 6.9 %collective-permute-start.5 = (bf16[96,3584]{1,0:T(8,128)(2,1)S(1)}, bf16[96,3584]{1,0:T(8,128)(2,1)S(1)}, u32[]{:S(2)}, u32[]{:S(2)}) collective-permute-start(bf16[96,3584]{1,0:T(8,128)(2,1)S(1)} %pad_maximum_fusion), channel_id=1, source_target_pairs={{0,1},{1,0},{2,3},{3,2},{4,5},{5,4},{6,7},{7,6},{8,9},{9,8},{10,11... | collective-permute-start | bytes 2064392 | tf_op jit(solution)/shard_map/ppermute | solution.py:66
  20.2 5.2 %collective-permute-start.4 = (bf16[32,3584]{1,0:T(8,128)(2,1)S(1)}, bf16[32,3584]{1,0:T(8,128)(2,1)S(1)}, u32[]{:S(2)}, u32[]{:S(2)}) collective-permute-start(bf16[32,3584]{1,0:T(8,128)(2,1)S(1)} %collective-permute-done.1), channel_id=1, source_target_pairs={{0,2},{2,4},{4,6},{6,8},{8,10},{10,12},{12,14},{14,0},{1,15},{3,1}... | collective-permute-start | bytes 688136 | tf_op jit(solution)/shard_map/ppermute | solution.py:69
  22.0 7.1 %collective-permute-start.6 = (bf16[32,3584]{1,0:T(8,128)(2,1)S(1)}, bf16[32,3584]{1,0:T(8,128)(2,1)S(1)}, u32[]{:S(2)}, u32[]{:S(2)}) collective-permute-start(bf16[32,3584]{1,0:T(8,128)(2,1)S(1)} %collective-permute-done.2), channel_id=1, source_target_pairs={{0,2},{2,4},{4,6},{6,8},{8,10},{10,12},{12,14},{14,0},{1,15},{3,1}... | collective-permute-start | bytes 688136 | tf_op jit(solution)/shard_map/ppermute | solution.py:69
  22.7 8.6 %collective-permute-start.7 = (bf16[32,3584]{1,0:T(8,128)(2,1)S(1)}, bf16[32,3584]{1,0:T(8,128)(2,1)S(1)}, u32[]{:S(2)}, u32[]{:S(2)}) collective-permute-start(bf16[32,3584]{1,0:T(8,128)(2,1)S(1)} %collective-permute-done.3), channel_id=1, source_target_pairs={{0,2},{2,4},{4,6},{6,8},{8,10},{10,12},{12,14},{14,0},{1,15},{3,1}... | collective-permute-start | bytes 688136 | tf_op jit(solution)/shard_map/ppermute | solution.py:69
  31.3 9.9 %collective-permute-start.9 = (bf16[96,3584]{1,0:T(8,128)(2,1)S(1)}, bf16[96,3584]{1,0:T(8,128)(2,1)S(1)}, u32[]{:S(2)}, u32[]{:S(2)}) collective-permute-start(bf16[96,3584]{1,0:T(8,128)(2,1)S(1)} %pad_maximum_fusion.1), channel_id=1, source_target_pairs={{0,1},{1,0},{2,3},{3,2},{4,5},{5,4},{6,7},{7,6},{8,9},{9,8},{10,11... | collective-permute-start | bytes 2064392 | tf_op jit(solution)/shard_map/ppermute | solution.py:66
  33.6 5.2 %collective-permute-start.8 = (bf16[32,3584]{1,0:T(8,128)(2,1)S(1)}, bf16[32,3584]{1,0:T(8,128)(2,1)S(1)}, u32[]{:S(2)}, u32[]{:S(2)}) collective-permute-start(bf16[32,3584]{1,0:T(8,128)(2,1)S(1)} %collective-permute-done.4), channel_id=1, source_target_pairs={{0,2},{2,4},{4,6},{6,8},{8,10},{10,12},{12,14},{14,0},{1,15},{3,1}... | collective-permute-start | bytes 688136 | tf_op jit(solution)/shard_map/ppermute | solution.py:69
  34.2 8.4 %collective-permute-start.10 = (bf16[32,3584]{1,0:T(8,128)(2,1)S(1)}, bf16[32,3584]{1,0:T(8,128)(2,1)S(1)}, u32[]{:S(2)}, u32[]{:S(2)}) collective-permute-start(bf16[32,3584]{1,0:T(8,128)(2,1)S(1)} %collective-permute-done.6), channel_id=1, source_target_pairs={{0,2},{2,4},{4,6},{6,8},{8,10},{10,12},{12,14},{14,0},{1,15},{3,1}... | collective-permute-start | bytes 688136 | tf_op jit(solution)/shard_map/ppermute | solution.py:69
  34.8 9.4 %collective-permute-start.12 = (bf16[32,3584]{1,0:T(8,128)(2,1)S(1)}, bf16[32,3584]{1,0:T(8,128)(2,1)S(1)}, u32[]{:S(2)}, u32[]{:S(2)}) collective-permute-start(bf16[32,3584]{1,0:T(8,128)(2,1)S(1)} %collective-permute-done.7), channel_id=1, source_target_pairs={{0,2},{2,4},{4,6},{6,8},{8,10},{10,12},{12,14},{14,0},{1,15},{3,1}... | collective-permute-start | bytes 688136 | tf_op jit(solution)/shard_map/ppermute | solution.py:69
  46.0 5.5 %collective-permute-start.15 = (bf16[128,3584]{1,0:T(8,128)(2,1)S(1)}, bf16[128,3584]{1,0:T(8,128)(2,1)S(1)}, u32[]{:S(2)}, u32[]{:S(2)}) collective-permute-start(bf16[128,3584]{1,0:T(8,128)(2,1)S(1)} %slice.73), channel_id=1, source_target_pairs={{0,1},{1,0},{2,3},{3,2},{4,5},{5,4},{6,7},{7,6},{8,9},{9,8},{10,11... | collective-permute-start | bytes 2752520 | tf_op jit(solution)/shard_map/ppermute | solution.py:66
  48.0 6.2 %collective-permute-start.17 = (bf16[16,3584]{1,0:T(8,128)(2,1)S(1)}, bf16[16,3584]{1,0:T(8,128)(2,1)S(1)}, u32[]{:S(2)}, u32[]{:S(2)}) collective-permute-start(bf16[16,3584]{1,0:T(8,128)(2,1)S(1)} %slice.75), channel_id=1, source_target_pairs={{0,2},{2,4},{4,6},{6,8},{8,10},{10,12},{12,14},{14,0},{1,15},{3,1}... | collective-permute-start | bytes 344072 | tf_op jit(solution)/shard_map/ppermute | solution.py:69
  65.6 5.5 %collective-permute-start.23 = (bf16[16,3584]{1,0:T(8,128)(2,1)S(1)}, bf16[16,3584]{1,0:T(8,128)(2,1)S(1)}, u32[]{:S(2)}, u32[]{:S(2)}) collective-permute-start(bf16[16,3584]{1,0:T(8,128)(2,1)S(1)} %shard_map.67), channel_id=1, source_target_pairs={{0,2},{2,4},{4,6},{6,8},{8,10},{10,12},{12,14},{14,0},{1,15},{3,1}... | collective-permute-start | bytes 344072 | tf_op jit(solution)/shard_map/ppermute | solution.py:69
  68.0 5.2 %collective-permute-start.24 = (bf16[32,3584]{1,0:T(8,128)(2,1)S(1)}, bf16[32,3584]{1,0:T(8,128)(2,1)S(1)}, u32[]{:S(2)}, u32[]{:S(2)}) collective-permute-start(bf16[32,3584]{1,0:T(8,128)(2,1)S(1)} %shard_map.68), channel_id=1, source_target_pairs={{0,2},{2,4},{4,6},{6,8},{8,10},{10,12},{12,14},{14,0},{1,15},{3,1}... | collective-permute-start | bytes 688136 | tf_op jit(solution)/shard_map/ppermute | solution.py:69
  70.1 6.2 %collective-permute-start.25 = (bf16[32,3584]{1,0:T(8,128)(2,1)S(1)}, bf16[32,3584]{1,0:T(8,128)(2,1)S(1)}, u32[]{:S(2)}, u32[]{:S(2)}) collective-permute-start(bf16[32,3584]{1,0:T(8,128)(2,1)S(1)} %shard_map.69), channel_id=1, source_target_pairs={{0,2},{2,4},{4,6},{6,8},{8,10},{10,12},{12,14},{14,0},{1,15},{3,1}... | collective-permute-start | bytes 688136 | tf_op jit(solution)/shard_map/ppermute | solution.py:69
  71.2 7.5 %collective-permute-start.26 = (bf16[32,3584]{1,0:T(8,128)(2,1)S(1)}, bf16[32,3584]{1,0:T(8,128)(2,1)S(1)}, u32[]{:S(2)}, u32[]{:S(2)}) collective-permute-start(bf16[32,3584]{1,0:T(8,128)(2,1)S(1)} %shard_map.70), channel_id=1, source_target_pairs={{0,2},{2,4},{4,6},{6,8},{8,10},{10,12},{12,14},{14,0},{1,15},{3,1}... | collective-permute-start | bytes 688136 | tf_op jit(solution)/shard_map/ppermute | solution.py:69
  73.3 7.9 %collective-permute-start.27 = (bf16[32,3584]{1,0:T(8,128)(2,1)S(1)}, bf16[32,3584]{1,0:T(8,128)(2,1)S(1)}, u32[]{:S(2)}, u32[]{:S(2)}) collective-permute-start(bf16[32,3584]{1,0:T(8,128)(2,1)S(1)} %shard_map.71), channel_id=1, source_target_pairs={{0,2},{2,4},{4,6},{6,8},{8,10},{10,12},{12,14},{14,0},{1,15},{3,1}... | collective-permute-start | bytes 688136 | tf_op jit(solution)/shard_map/ppermute | solution.py:69
  76.4 6.7 %collective-permute-start.28 = (bf16[32,3584]{1,0:T(8,128)(2,1)S(1)}, bf16[32,3584]{1,0:T(8,128)(2,1)S(1)}, u32[]{:S(2)}, u32[]{:S(2)}) collective-permute-start(bf16[32,3584]{1,0:T(8,128)(2,1)S(1)} %shard_map.72), channel_id=1, source_target_pairs={{0,2},{2,4},{4,6},{6,8},{8,10},{10,12},{12,14},{14,0},{1,15},{3,1}... | collective-permute-start | bytes 688136 | tf_op jit(solution)/shard_map/ppermute | solution.py:69
  78.8 7.4 %collective-permute-start.29 = (bf16[32,3584]{1,0:T(8,128)(2,1)S(1)}, bf16[32,3584]{1,0:T(8,128)(2,1)S(1)}, u32[]{:S(2)}, u32[]{:S(2)}) collective-permute-start(bf16[32,3584]{1,0:T(8,128)(2,1)S(1)} %shard_map.73), channel_id=1, source_target_pairs={{0,2},{2,4},{4,6},{6,8},{8,10},{10,12},{12,14},{14,0},{1,15},{3,1}... | collective-permute-start | bytes 688136 | tf_op jit(solution)/shard_map/ppermute | solution.py:69
  83.1 5.8 %collective-permute-start.30 = (bf16[32,3584]{1,0:T(8,128)(2,1)S(1)}, bf16[32,3584]{1,0:T(8,128)(2,1)S(1)}, u32[]{:S(2)}, u32[]{:S(2)}) collective-permute-start(bf16[32,3584]{1,0:T(8,128)(2,1)S(1)} %shard_map.74), channel_id=1, source_target_pairs={{0,2},{2,4},{4,6},{6,8},{8,10},{10,12},{12,14},{14,0},{1,15},{3,1}... | collective-permute-start | bytes 688136 | tf_op jit(solution)/shard_map/ppermute | solution.py:69
  86.0 5.3 %collective-permute-start.31 = (bf16[32,3584]{1,0:T(8,128)(2,1)S(1)}, bf16[32,3584]{1,0:T(8,128)(2,1)S(1)}, u32[]{:S(2)}, u32[]{:S(2)}) collective-permute-start(bf16[32,3584]{1,0:T(8,128)(2,1)S(1)} %shard_map.75), channel_id=1, source_target_pairs={{0,2},{2,4},{4,6},{6,8},{8,10},{10,12},{12,14},{14,0},{1,15},{3,1}... | collective-permute-start | bytes 688136 | tf_op jit(solution)/shard_map/ppermute | solution.py:69
  86.4 7.5 %collective-permute-start.32 = (bf16[32,3584]{1,0:T(8,128)(2,1)S(1)}, bf16[32,3584]{1,0:T(8,128)(2,1)S(1)}, u32[]{:S(2)}, u32[]{:S(2)}) collective-permute-start(bf16[32,3584]{1,0:T(8,128)(2,1)S(1)} %shard_map.76), channel_id=1, source_target_pairs={{0,2},{2,4},{4,6},{6,8},{8,10},{10,12},{12,14},{14,0},{1,15},{3,1}... | collective-permute-start | bytes 688136 | tf_op jit(solution)/shard_map/ppermute | solution.py:69
  93.8 7.5 %collective-permute-start.33 = (bf16[16,3584]{1,0:T(8,128)(2,1)S(1)}, bf16[16,3584]{1,0:T(8,128)(2,1)S(1)}, u32[]{:S(2)}, u32[]{:S(2)}) collective-permute-start(bf16[16,3584]{1,0:T(8,128)(2,1)S(1)} %shard_map.77), channel_id=1, source_target_pairs={{0,1},{1,0},{2,3},{3,2},{4,5},{5,4},{6,7},{7,6},{8,9},{9,8},{10,11... | collective-permute-start | bytes 344072 | tf_op jit(solution)/shard_map/ppermute | solution.py:66
  (18 other events, 69.2 us)
